TPU v7x, 512 devices: a whole 4x8x8 slice. The times are simulated.
512 devices in a mesh: expert: 128 (over x, z, y_hi, core), replica: 4 (over y_lo).
Axes of the slice: x: 4, y: 8 (y_hi: 2, y_lo: 4; y = y_hi * 4 + y_lo), z: 8, core: 2. Of those that a mesh axis runs over, the one named last changes fastest.
Arguments:
- tokens: bfloat16 [65536, 2048], P(('replica', 'expert')), parts along dimension 0, may hold values from -6 to 6
- expert_ids: int32 [65536, 8], P(('replica', 'expert')), parts along dimension 0, may hold values from 0 to 127, all different within a row; in each aligned block of 128 rows (0 to 127, 128 to 255, ...) at most 12 rows name the same one
- combine: float32 [65536, 8], P(('replica', 'expert')), parts along dimension 0, may hold values from 0.25 to 1
- old_gate: bfloat16 [24576, 2048], P('expert'), may hold values from -0.125 to 0.125
- old_up: bfloat16 [24576, 2048], P('expert'), may hold values from -0.125 to 0.125
- old_down: bfloat16 [24576, 2048], P('expert'), may hold values from -0.21875 to 0.21875
- move_plan: int32 [32, 3, 96], replicated, may hold values from -1 to 191, as said below
Outputs:
- mixed: bfloat16 [65536, 2048], P(('replica', 'expert')), parts along dimension 0
- arrived: bfloat16 [12, 12288, 2048], P('replica', 'expert'), parts along dimension 0
There are 4 independent parts, one for each index of `replica`. A program takes and returns all parts, laid end to end along the dimension named above; an argument that names none is the same for every part. Nothing has to cross between parts.
Inputs may be any that keep to these rules, and one draw needn't show every extreme that they name: `expert_ids`: each row names 8 different experts; among the 128 rows of one device no expert is named more than 12 times, a bound that some block reaches. `move_plan`: in each group the non-negative entries over the three survivors name every one of the leaving device's 192 rows exactly once; each survivor's entries fill its slots from the first, -1 after them; every survivor receives at least 24 rows; in every draw some survivor receives 96 rows.
All inputs are finite; a program needn't handle non-finite values.
Results may differ from a plain program's by a relative error of at most 0.0058.
Values may be sent and summed in bfloat16 or wider, within the bound.
A program may use at most 128 MiB of HBM per device.

v0:
```python
import jax
import jax.numpy as jnp
from jax import lax
from jax.sharding import PartitionSpec as P

CAP = 12


def shifted(block, axis, distance):
    devices = range(lax.axis_size(axis))
    route = [(i - distance, i) for i in devices if i - distance in devices]
    return lax.ppermute(block, axis, route)


def project(row_block, weights):
    numbers = (((1,), (1,)), ((), ()))
    gate_value = lax.dot_general(row_block, weights[0], numbers, preferred_element_type=jnp.float32)
    up_value = lax.dot_general(row_block, weights[1], numbers, preferred_element_type=jnp.float32)
    hidden = (jax.nn.silu(gate_value) * up_value).astype(jnp.bfloat16)
    return jnp.dot(hidden, weights[2], preferred_element_type=jnp.float32)


def select_rows(resident, plan_row):
    gathered = jnp.take(resident, jnp.maximum(plan_row, 0), axis=1)
    return jnp.where((plan_row >= 0)[None, :, None], gathered, jnp.zeros((), resident.dtype))


def on_device(tokens, expert_ids, combine, old_gate, old_up, old_down, move_plan):
    device_index = lax.axis_index("expert")
    group_index = device_index // 4
    position = device_index % 4
    resident = jnp.stack([old_gate, old_up, old_down], axis=0)
    group_plan = lax.dynamic_index_in_dim(move_plan, group_index, 0, keepdims=False)
    leaving = position == 3
    arrived = jnp.zeros((3, move_plan.shape[2], resident.shape[2]), resident.dtype)
    for offset in (1, 2, 3):
        parcel = jnp.where(
            leaving, select_rows(resident, group_plan[3 - offset]), jnp.zeros((), resident.dtype)
        )
        landed = shifted(parcel, "expert", -offset)
        arrived = arrived + landed
    tok_count, top_count = expert_ids.shape
    model_width = tokens.shape[1]
    experts_here = move_plan.shape[0]
    slot_total = experts_here * CAP
    flat_ids = expert_ids.reshape(-1)
    in_window = flat_ids < experts_here
    onehot = (flat_ids[:, None] == jnp.arange(experts_here, dtype=jnp.int32)[None, :]).astype(
        jnp.int32
    )
    slot_rank = jnp.sum(jnp.cumsum(onehot, axis=0) * onehot, axis=1) - 1
    slot_index = jnp.where(in_window, flat_ids * CAP + slot_rank, slot_total)
    source_token = (
        jnp.zeros((slot_total,), jnp.int32)
        .at[slot_index]
        .set(jnp.arange(flat_ids.shape[0], dtype=jnp.int32) // top_count, mode="drop")
    )
    filled = jnp.zeros((slot_total,), jnp.bool_).at[slot_index].set(True, mode="drop")
    slot_token_rows = jnp.where(
        filled[:, None], jnp.take(tokens, source_token, axis=0), jnp.zeros((), tokens.dtype)
    )
    slot_token_rows = slot_token_rows.reshape(experts_here, CAP, model_width)
    held_rows = jnp.concatenate([resident, arrived], axis=1)
    remaining_device = (jnp.arange(4) < 3).reshape(1, 4, 1, 1)
    departing_rows = jnp.where(
        remaining_device, slot_token_rows[:, None], jnp.zeros((), tokens.dtype)
    ).reshape(experts_here * 4, CAP, model_width)
    incoming = lax.all_to_all(departing_rows, "expert", split_axis=0, concat_axis=0, tiled=True)
    sources = incoming.shape[0]
    slot_count = incoming.shape[1]
    row_block = incoming.reshape(sources * slot_count, model_width)
    partial_value = (
        project(row_block, held_rows).astype(jnp.bfloat16).reshape(sources, slot_count, model_width)
    )
    returned = lax.all_to_all(partial_value, "expert", split_axis=0, concat_axis=0, tiled=True)
    summed = jnp.sum(
        returned.reshape(experts_here, 4, CAP, model_width)[:, :3].astype(jnp.float32), axis=1
    )
    weight_flat = jnp.where(in_window, combine.reshape(-1), jnp.zeros((), combine.dtype))
    picked = jnp.take(
        summed.reshape(slot_total, model_width), jnp.minimum(slot_index, slot_total - 1), axis=0
    )
    mixed = jnp.sum(
        (picked * weight_flat[:, None]).reshape(tok_count, top_count, model_width), axis=1
    )
    return (mixed.astype(jnp.bfloat16), arrived)


def solution(mesh):
    placed = (
        P(("replica", "expert"), None),
        P(("replica", "expert"), None),
        P(("replica", "expert"), None),
        P("expert", None),
        P("expert", None),
        P("expert", None),
        P(),
    )
    return jax.shard_map(
        on_device,
        mesh=mesh,
        in_specs=placed,
        out_specs=(P(("replica", "expert"), None), P("replica", "expert", None)),
        check_vma=False,
    )
```

profile of v0, /device:TPU:8, one launch (start us, length us, event | category | flops | bytes accessed | tf_op | source)
XLA Modules:
  0.0 651.0 jit_solution(8513538935524039934)
XLA Ops:
  0.7 0.7 broadcast_multiply_fusion
  1.4 0.8 copy.47
  2.6 9.0 %reduce-window.6 = s32[32,8,128]{2,1,0:T(8,128)S(1)} reduce-window(s32[32,8,128]{2,1,0:T(8,128)S(1)} %fusion.17, s32[]{:T(128)} %constant.100.clone.1), window={size=1x1x128 pad=0_0x0_0x127_0}, to_apply=%region_0.1 | reduce-window | flops 4161536 | bytes 262148 | tf_op jit(solution)/shard_map/reduce-window
  11.7 0.1 copy.49
  12.3 0.7 compare_and_fusion
  13.0 0.1 copy.53
  13.2 4.3 scatter_custom_fusion.1
  17.8 4.3 scatter_custom_fusion
  22.3 3.1 gather_fusion
  25.4 2.4 gather.16
  27.8 0.3 select_select_fusion
  28.1 3.8 bitcast_select_fusion.1
  32.0 20.2 %all-to-all-start = ((bf16[128,12,2048]{2,1,0:T(8,128)(2,1)}), bf16[128,12,2048]{2,1,0:T(8,128)(2,1)}, u32[]{:S(2)}, u32[]{:S(2)}) async-start(bf16[128,12,2048]{2,1,0:T(8,128)(2,1)} %bitcast_select_fusion.1), calls=%async_computation | async-start | bytes 16777216 | tf_op jit(solution)/shard_map/all_to_all | solution.py:68
  52.3 2.4 copy.55
  54.7 2.4 copy.56
  57.0 2.4 copy.57
  59.4 0.7 compare_and_fusion.3
  60.2 6.8 %pad_maximum_fusion.1 = bf16[3,192,2048]{2,0,1:T(4,128)(2,1)S(1)} fusion(bf16[1,192,2048]{2,0,1:T(2,128)(2,1)} %copy.57, bf16[1,192,2048]{2,0,1:T(2,128)(2,1)} %copy.56, bf16[1,192,2048]{2,0,1:T(2,128)(2,1)} %copy.55), kind=kLoop, calls=%fused_computation.14 | loop fusion | flops 7077888 | bytes 4718592 | tf_op jit(solution)/shard_map/stack | solution.py:32
  67.0 3.1 gather_fusion.4
  70.1 0.7 compare_bitcast_fusion.2
  70.9 2.8 fusion.3
  73.6 1.9 copy.62
  75.5 1.5 collective-permute-start.2
  77.1 3.1 gather_fusion.3
  80.2 2.8 fusion.4
  82.9 2.0 copy.59
  84.9 1.3 collective-permute-start.1
  86.2 3.1 gather_fusion.2
  89.4 2.8 fusion.5
  92.1 0.9 copy.58
  93.0 2.0 collective-permute-start
  95.0 220.1 %collective-permute-done.2 = bf16[3,96,2048]{2,1,0:T(8,128)(2,1)} collective-permute-done((bf16[3,96,2048]{2,1,0:T(8,128)(2,1)}, bf16[3,96,2048]{2,1,0:T(8,128)(2,1)}, u32[]{:S(2)}, u32[]{:S(2)}) %collective-permute-start.2) | collective-permute-done | bytes 1179680 | tf_op jit(solution)/shard_map/ppermute | solution.py:12
  315.1 0.7 collective-permute-done.1
  315.8 8.0 %copy_add_fusion = bf16[3,96,2048]{2,0,1:T(4,128)(2,1)S(1)} fusion(bf16[3,96,2048]{2,1,0:T(8,128)(2,1)} %collective-permute-done.2, bf16[3,96,2048]{2,1,0:T(8,128)(2,1)} %collective-permute-done.1, bf16[3,96,2048]{2,1,0:T(8,128)(2,1)S(1)} %collective-permute-done), kind=kLoop, calls=%fused_computation.24 | loop fusion | flops 1179648 | bytes 4718592 | tf_op jit(solution)/shard_map/add | solution.py:41
  323.8 6.5 pad_maximum_fusion
  330.3 6.4 fusion.26
  336.7 10.8 %reshape.208 = bf16[1536,2048]{1,0:T(8,128)(2,1)} reshape(bf16[128,12,2048]{2,1,0:T(8,128)(2,1)} %all-to-all-done) | data formatting | bytes 12582912 | tf_op jit(solution)/shard_map/reshape | solution.py:71
  347.5 7.0 %fusion.10 = f32[1536,288]{0,1:T(8,128)} fusion(bf16[1536,2048]{1,0:T(8,128)(2,1)} %reshape.208, bf16[1,288,2048]{2,0,1:T(2,128)(2,1)} %get-tuple-element.21), kind=kOutput, calls=%fused_computation.30 | convolution fusion | flops 1811939328 | bytes 9240576 | tf_op jit(solution)/shard_map/dot_general | solution.py:17
  354.5 13.1 %convolution_convert_fusion = bf16[1536,2048]{1,0:T(8,128)(2,1)} fusion(bf16[1,288,2048]{2,0,1:T(2,128)(2,1)} %get-tuple-element.20, bf16[1536,2048]{1,0:T(8,128)(2,1)} %reshape.208, f32[1536,288]{0,1:T(8,128)} %fusion.10, bf16[1,288,2048]{2,0,1:T(2,128)(2,1)} %get-tuple-element.19), kind=kOutput, calls=%fused_computation.12 | convolution fusion | flops 3629678592 | bytes 16711680 | tf_op jit(solution)/shard_map/dot_general | solution.py:20
  367.7 10.6 %reshape.209 = bf16[128,12,2048]{2,1,0:T(8,128)(2,1)} reshape(bf16[1536,2048]{1,0:T(8,128)(2,1)} %convolution_convert_fusion) | data formatting | bytes 12582912 | tf_op jit(solution)/shard_map/reshape | solution.py:73
  378.3 54.5 %all-to-all-start.1 = ((bf16[128,12,2048]{2,1,0:T(8,128)(2,1)}), bf16[128,12,2048]{2,1,0:T(8,128)(2,1)}, u32[]{:S(2)}, u32[]{:S(2)}) async-start(bf16[128,12,2048]{2,1,0:T(8,128)(2,1)} %reshape.209), calls=%async_computation.1 | async-start | bytes 16777216 | tf_op jit(solution)/shard_map/all_to_all | solution.py:75
  432.8 0.1 copy.52
  433.1 1.9 copy.65
  434.9 192.6 %all-to-all-done.1 = bf16[128,12,2048]{2,1,0:T(8,128)(2,1)} async-done(((bf16[128,12,2048]{2,1,0:T(8,128)(2,1)}), bf16[128,12,2048]{2,1,0:T(8,128)(2,1)}, u32[]{:S(2)}, u32[]{:S(2)}) %all-to-all-start.1) | async-done | bytes 6291488 | tf_op jit(solution)/shard_map/all_to_all | solution.py:75
  627.6 6.7 %convert_reduce_fusion = f32[32,12,2048]{2,1,0:T(8,128)} fusion(bf16[32,4,12,2048]{3,2,1,0:T(8,128)(2,1)} %bitcast.17), kind=kLoop, calls=%fused_computation.7 | loop fusion | flops 3932160 | bytes 7864320 | tf_op jit(solution)/shard_map/reduce_sum | solution.py:76
  634.2 3.0 reshape.211
  637.2 6.8 %gather_fusion.1 = f32[1024,2048]{1,0:T(8,128)} fusion(f32[384,2048]{1,0:T(8,128)S(1)} %reshape.211, s32[1024]{0:T(1024)S(1)} %broadcast_clamp_fusion), kind=kCustom, calls=%fused_computation.4 | custom fusion | bytes 16781312 | tf_op jit(solution)/shard_map/jit(_take)/gather | solution.py:80
  644.0 6.8 %fusion.1 = bf16[128,2048]{1,0:T(8,128)(2,1)} fusion(f32[1024,2048]{1,0:T(8,128)} %gather_fusion.1, f32[128,8]{1,0:T(8,128)S(1)} %copy.64, pred[128,8]{1,0:T(8,128)(4,1)S(1)} %copy.52), kind=kLoop, calls=%fused_computation.10 | loop fusion | flops 6029312 | bytes 8918016 | tf_op jit(solution)/shard_map/reduce_sum | solution.py:83
  (52 shorter events, 1.5 us)
Async XLA Ops:
  0.6 21.7 %copy-start = (bf16[128,2048]{1,0:T(8,128)(2,1)S(1)}, bf16[128,2048]{1,0:T(8,128)(2,1)}, u32[]{:S(2)}) copy-start(bf16[128,2048]{1,0:T(8,128)(2,1)} %param.9) | copy-start | bytes 1572868
  32.0 20.3 %copy-start.5 = (bf16[192,2048]{1,0:T(8,128)(2,1)S(1)}, bf16[192,2048]{1,0:T(8,128)(2,1)}, u32[]{:S(2)}) copy-start(bf16[192,2048]{1,0:T(8,128)(2,1)} %param.12) | copy-start | bytes 2359300
  32.0 304.7 %all-to-all-start = ((bf16[128,12,2048]{2,1,0:T(8,128)(2,1)}), bf16[128,12,2048]{2,1,0:T(8,128)(2,1)}, u32[]{:S(2)}, u32[]{:S(2)}) async-start(bf16[128,12,2048]{2,1,0:T(8,128)(2,1)} %bitcast_select_fusion.1), calls=%async_computation | async-start | bytes 16777216 | tf_op jit(solution)/shard_map/all_to_all | solution.py:68
  52.2 2.4 copy-start.6
  52.3 4.8 copy-start.7
  75.5 239.6 %collective-permute-start.2 = (bf16[3,96,2048]{2,1,0:T(8,128)(2,1)}, bf16[3,96,2048]{2,1,0:T(8,128)(2,1)}, u32[]{:S(2)}, u32[]{:S(2)}) collective-permute-start(bf16[3,96,2048]{2,1,0:T(8,128)(2,1)} %copy.62), channel_id=1, source_target_pairs={{12,0},{16,4},{20,8},{24,12},{28,16},{32,20},{36,24},{40,28},{44,3... | collective-permute-start | bytes 3538952 | tf_op jit(solution)/shard_map/ppermute | solution.py:12
  84.9 230.8 %collective-permute-start.1 = (bf16[3,96,2048]{2,1,0:T(8,128)(2,1)}, bf16[3,96,2048]{2,1,0:T(8,128)(2,1)}, u32[]{:S(2)}, u32[]{:S(2)}) collective-permute-start(bf16[3,96,2048]{2,1,0:T(8,128)(2,1)} %copy.59), channel_id=1, source_target_pairs={{8,0},{12,4},{16,8},{20,12},{24,16},{28,20},{32,24},{36,28},{40,32... | collective-permute-start | bytes 3538952 | tf_op jit(solution)/shard_map/ppermute | solution.py:12
  93.0 230.8 %copy-start.2 = (bf16[1,192,2048]{2,0,1:T(2,128)(2,1)S(1)}, bf16[1,192,2048]{2,0,1:T(2,128)(2,1)}, u32[]{:S(2)}) copy-start(bf16[1,192,2048]{2,0,1:T(2,128)(2,1)} %copy.55) | copy-start | bytes 2359300
  93.0 230.8 %copy-start.3 = (bf16[1,192,2048]{2,0,1:T(2,128)(2,1)S(1)}, bf16[1,192,2048]{2,0,1:T(2,128)(2,1)}, u32[]{:S(2)}) copy-start(bf16[1,192,2048]{2,0,1:T(2,128)(2,1)} %copy.56) | copy-start | bytes 2359300
  93.0 230.8 %copy-start.4 = (bf16[1,192,2048]{2,0,1:T(2,128)(2,1)S(1)}, bf16[1,192,2048]{2,0,1:T(2,128)(2,1)}, u32[]{:S(2)}) copy-start(bf16[1,192,2048]{2,0,1:T(2,128)(2,1)} %copy.57) | copy-start | bytes 2359300
  93.0 222.8 %collective-permute-start = (bf16[3,96,2048]{2,1,0:T(8,128)(2,1)S(1)}, bf16[3,96,2048]{2,1,0:T(8,128)(2,1)S(1)}, u32[]{:S(2)}, u32[]{:S(2)}) collective-permute-start(bf16[3,96,2048]{2,1,0:T(8,128)(2,1)S(1)} %copy.58), channel_id=1, source_target_pairs={{4,0},{8,4},{12,8},{16,12},{20,16},{24,20},{28,24},{32,28},{36,32}... | collective-permute-start | bytes 3538952 | tf_op jit(solution)/shard_map/ppermute | solution.py:12
  378.3 54.7 %copy-start.8 = (f32[128,8]{0,1:T(8,128)S(1)}, f32[128,8]{0,1:T(8,128)}, u32[]{:S(2)}) copy-start(f32[128,8]{0,1:T(8,128)} %param.11) | copy-start | bytes 12292
  378.3 249.3 %all-to-all-start.1 = ((bf16[128,12,2048]{2,1,0:T(8,128)(2,1)}), bf16[128,12,2048]{2,1,0:T(8,128)(2,1)}, u32[]{:S(2)}, u32[]{:S(2)}) async-start(bf16[128,12,2048]{2,1,0:T(8,128)(2,1)} %reshape.209), calls=%async_computation.1 | async-start | bytes 16777216 | tf_op jit(solution)/shard_map/all_to_all | solution.py:75
  644.0 6.8 %copy-start.1 = (bf16[128,2048]{1,0:T(8,128)(2,1)S(1)}, bf16[128,2048]{1,0:T(8,128)(2,1)}, u32[]{:S(2)}) copy-start(bf16[128,2048]{1,0:T(8,128)(2,1)} %param.9) | copy-start | bytes 1572868
where the time goes:
time: 660 us; the launch traced here: 651 us
  waiting for transfers between devices  413 us (63%)
  starting transfers between devices  79.6 us (12%)
  local copies, waits for them, and re-layouts  77.2 us (12%)
  other arithmetic  59.4 us (9%)
  matrix products  20.2 us (3%)
    ppermute x3, waiting for transfers between devices, shifted(): return lax.ppermute(block, axis, route)  221 us
    all_to_all x1, waiting for transfers between devices, on_device(): lax.all_to_all(partial_value, 'expert', split_axis=0, concat_axis=0, tile...  193 us
    all_to_all x1, starting transfers between devices, on_device(): lax.all_to_all(partial_value, 'expert', split_axis=0, concat_axis=0, tile...  54.5 us
    all_to_all x1, starting transfers between devices, on_device(): lax.all_to_all(departing_rows, 'expert', split_axis=0, concat_axis=0, til...  20.2 us
  transfers between devices with their start and end apart: 5, of which 3 were waited for; matrix products, arithmetic and copies ran while one was open for 9% of the time, Pallas kernels for 0%

commit v1 on v0

v1 whole, which is shorter than its diff:
```python
import jax
import jax.numpy as jnp
from jax import lax
from jax.experimental import pallas as pl
from jax.experimental.pallas import tpu as pltpu
from jax.sharding import PartitionSpec as P

MESH = pl.DeviceIdType.MESH
F32 = jnp.float32
BF16 = jnp.bfloat16

X, Z, RING, HALF = 4, 8, 8, 4
EXPERTS = X * Z
TOK = 128
D = 2048
Q = D // 4
WIDE = 3 * Q
CAP = 12
ROWS = 16
OLD = 192
UNITS = 4 * OLD
MOVE = 96
CHUNKS = 6
PIECE = 3 * OLD // 2 // CHUNKS
PER = CHUNKS // 3
BATCH = 16
NT = (((1,), (1,)), ((), ()))


def dot(a, b):
    return jnp.dot(a, b, preferred_element_type=F32)


def dot_nt(a, b):
    return lax.dot_general(a, b, NT, preferred_element_type=F32)


def one_hot(condition):
    return jnp.where(condition, 1.0, 0.0).astype(BF16)


def z_offset(k):
    odd = lax.rem(k, 2)
    return odd * lax.div(k + 1, 2) + (1 - odd) * lax.rem(Z - lax.div(k, 2), Z)


def kernel(
    tok, ids, comb, gate, up, down, plan, mixed, arrived,
    wts, send, recv, outs, ret, hid, x3, lhs, fold, arr,
    own_sem, d_send, d_recv, r_send, r_recv, cross_send, hop_send, hop_recv,
    side_send, side_recv, twin_send, twin_recv, arr_sem,
):
    e = lax.axis_index("expert")
    rep = lax.axis_index("replica")
    low, grp = lax.rem(e, 4), lax.div(e, 4)
    half, core = lax.div(low, 2), lax.rem(low, 2)
    gx, gz = lax.div(grp, Z), lax.rem(grp, Z)
    y = half * HALF + rep
    step = 2 * half - 1
    twin = (e + 1 - 2 * core, rep)

    def peer(o, sign):
        ox, oz = lax.div(o, Z), z_offset(lax.rem(o, Z))
        g = lax.rem(gx + X + sign * ox, X) * Z + lax.rem(gz + Z + sign * oz, Z)
        return (4 * g + low, rep)

    def ring(distance):
        there = lax.rem(y + RING + distance, RING)
        return (4 * grp + 2 * lax.div(there, HALF) + core, lax.rem(there, HALF))

    barrier = pltpu.get_barrier_semaphore()

    def greet(device):
        pl.semaphore_signal(barrier, inc=1, device_id=device, device_id_type=MESH)

    @pl.loop(1, EXPERTS)
    def _(o):
        greet(peer(o, 1))

    greet(twin)
    greet(ring(1))
    greet(ring(-1))

    mats = (gate, up, down)
    own = [
        pltpu.make_async_copy(mats[m], wts.at[m, pl.ds(pl.multiple_of(low * OLD, 16), OLD)], own_sem.at[m])
        for m in range(3)
    ]
    for copy in own:
        copy.start()

    ids_t = jnp.transpose(ids[...])
    row = lax.broadcasted_iota(jnp.int32, (128, 128), 0)
    lane = lax.broadcasted_iota(jnp.int32, (128, 128), 1)
    before = one_hot(row < lane)
    slot = row & 15

    def named(i):
        k = row >> 4
        oz = jnp.where((k & 1) == 1, (k + 1) >> 1, (8 - (k >> 1)) & 7)
        g = ((gx + i) & 3) * Z + ((gz + oz) & 7)
        return [ids_t[k : k + 1, :] == g for k in range(8)]

    def places(hits):
        member = hits[0]
        for hit in hits[1:]:
            member = member | hit
        rank = dot(one_hot(member), before)
        rank = jnp.where(member, rank, -1.0).astype(jnp.int32)
        first = (rank == slot) & (slot < CAP)
        last = [(rank == 3 * (slot - CAP) + b) & (slot >= CAP) for b in range(3)]
        return first, last

    @pl.loop(0, 4)
    def _(i):
        first, last = places(named(i))
        rows = pl.ds(pl.multiple_of(i * 128, 128), 128)
        first = one_hot(first)
        for b in range(3):
            part = dot(first, tok[:, b * Q : (b + 1) * Q]) + dot(one_hot(last[b]), tok[:, WIDE:])
            send[rows, b * Q : (b + 1) * Q] = part.astype(BF16)

    pl.semaphore_wait(barrier, EXPERTS + 2)

    def piece(owner, part, k):
        start = owner * OLD + part * (OLD // 2) + lax.rem(k, PER) * PIECE
        return wts.at[lax.div(k, PER), pl.ds(pl.multiple_of(start, 16), PIECE)]

    def passing(ref, sender, receiver, device):
        return pltpu.make_async_remote_copy(
            src_ref=ref, dst_ref=ref, send_sem=sender, recv_sem=receiver, device_id=device, device_id_type=MESH
        )

    position = (half * rep + (1 - half) * (HALF - 1 - rep), half * (HALF - 1 - rep) + (1 - half) * rep)
    ahead = (ring(step), ring(-step))
    behind = (ring(-step), ring(step))
    far = lax.rem(low + 2, 4)

    def cross(part, k):
        return passing(piece(low, part, k), cross_send.at[part, k], hop_recv.at[part, k], behind[part])

    def hop(part, k):
        return passing(piece(far, part, k), hop_send.at[part, k], hop_recv.at[part, k], ahead[part])

    def side(part, k, owner):
        return passing(piece(owner, part, k), side_send.at[part, k], side_recv.at[part, k], twin)

    def own_side(m, owner):
        ref = wts.at[m, pl.ds(pl.multiple_of(owner * OLD, 16), OLD)]
        return passing(ref, twin_send.at[m], twin_recv.at[m], twin)

    for copy in own:
        copy.wait()

    for part in range(2):
        @pl.when(position[part] == 0)
        def _():
            @pl.loop(0, CHUNKS)
            def _(k):
                cross(part, k).start()

    def parcel(source, target, o, sender, receiver, device):
        rows = pl.ds(pl.multiple_of(o * ROWS, ROWS), ROWS)
        return pltpu.make_async_remote_copy(
            src_ref=source.at[rows], dst_ref=target.at[rows], send_sem=sender.at[o], recv_sem=receiver.at[o],
            device_id=device, device_id_type=MESH,
        )

    def dispatch(o):
        return parcel(send, recv, o, d_send, d_recv, peer(o, 1))

    def give_back(o):
        return parcel(outs, ret, o, r_send, r_recv, peer(o, -1))

    @pl.loop(1, EXPERTS)
    def _(o):
        dispatch(o).start()

    for m in range(3):
        own_side(m, low).start()

    recv[0:ROWS, :] = send[0:ROWS, :]

    comb_t = jnp.transpose(comb[...])

    @pl.loop(0, 4)
    def _(i):
        hits = named(i)
        first, last = places(hits)
        weight = jnp.zeros((128, 128), F32)
        for k in range(8):
            weight = weight + jnp.where(hits[k], comb_t[k : k + 1, :], 0.0)
        columns = pl.ds(pl.multiple_of(i * 128, 128), 128)

        def store(b, at, chosen):
            value = jnp.transpose(jnp.where(chosen, weight, 0.0))
            high = value.astype(BF16)
            lhs[b, at : at + 128, columns] = high
            lhs[b, at + 128 : at + 256, columns] = (value - high.astype(F32)).astype(BF16)

        for b in range(3):
            store(b, 0, first)
            store(b, 256, last[b])

    n_rows = BATCH * ROWS
    low_row = lax.broadcasted_iota(jnp.int32, (n_rows, n_rows), 0)
    high_row = lax.broadcasted_iota(jnp.int32, (n_rows, n_rows), 1)
    same = (low_row >> 4) == (high_row >> 4)
    for b in range(3):
        fold[b] = one_hot(
            same & ((low_row & 15) >= CAP) & ((high_row & 15) == 3 * ((low_row & 15) - CAP) + b)
        )
        fold[3 + b] = one_hot(
            same & ((high_row & 15) >= CAP) & ((low_row & 15) == 3 * ((high_row & 15) - CAP) + b)
        )

    @pl.loop(0, CHUNKS + HALF - 1)
    def _(j):
        for part in range(2):
            k = j - position[part]

            @pl.when((k >= 0) & (k < CHUNKS))
            def _():
                hop(part, k).wait_recv()

                @pl.when(position[part] < HALF - 1)
                def _():
                    hop(part, k).start()

                side(part, k, far).start()

    for m in range(3):
        own_side(m, lax.rem(low + 1, 2) + 2 * half).wait_recv()

    @pl.loop(0, CHUNKS)
    def _(k):
        for part in range(2):
            side(part, k, lax.rem(far + 1, 2) + 2 * (1 - half)).wait_recv()

    out_slot = lax.broadcasted_iota(jnp.int32, (n_rows, Q), 0) & 15

    @pl.loop(0, EXPERTS // BATCH)
    def _(i):
        @pl.loop(0, BATCH)
        def _(j):
            o = i * BATCH + j

            @pl.when(o > 0)
            def _():
                dispatch(o).wait_recv()

        rows = pl.ds(pl.multiple_of(i * n_rows, n_rows), n_rows)
        tail = dot(fold[3], recv[rows, 0:Q])
        for b in range(1, 3):
            tail = tail + dot(fold[3 + b], recv[rows, b * Q : (b + 1) * Q])
        x3[...] = tail.astype(BF16)

        @pl.loop(0, UNITS // 256)
        def _(n):
            units = pl.ds(pl.multiple_of(n * 256, 256), 256)

            def project(m):
                return dot_nt(recv[rows, :], wts[m, units, 0:WIDE]) + dot_nt(x3[...], wts[m, units, WIDE:])

            gate_value = project(0)
            hidden = gate_value / (1.0 + jnp.exp(-gate_value)) * project(1)
            hid[:, units] = hidden.astype(BF16)

        last = dot(hid[...], wts[2, :, WIDE:]).astype(BF16)
        for b in range(3):
            columns = slice(b * Q, (b + 1) * Q)
            value = dot(hid[...], wts[2, :, columns])
            outs[rows, columns] = jnp.where(out_slot < CAP, value, dot(fold[b], last)).astype(BF16)

        @pl.loop(0, BATCH)
        def _(j):
            o = i * BATCH + j

            @pl.when(o > 0)
            def _():
                give_back(o).start()

    ret[0:ROWS, :] = outs[0:ROWS, :]

    mine = plan[grp, pl.ds(lax.rem(low, 3), 1), :]
    wanted = lax.broadcasted_iota(jnp.int32, (OLD, MOVE), 0) == mine
    chosen = jnp.transpose(jnp.where(wanted, jnp.where(low < 3, 1.0, 0.0), 0.0)).astype(BF16)
    for m in range(3):
        for b in range(4):
            columns = slice(b * Q, (b + 1) * Q)
            arr[m, :, columns] = dot(chosen, wts[m, 3 * OLD : 4 * OLD, columns]).astype(BF16)
    arr_copy = pltpu.make_async_copy(arr, arrived, arr_sem)
    arr_copy.start()

    @pl.loop(1, EXPERTS)
    def _(o):
        give_back(o).wait_recv()

    end = jnp.zeros((TOK, Q), F32)
    for b in range(3):
        columns = slice(b * Q, (b + 1) * Q)
        sums = dot(lhs[b], ret[:, columns])
        mixed[:, columns] = (sums[0:128] + sums[128:256]).astype(BF16)
        end = end + (sums[256:384] + sums[384:512])
    mixed[:, WIDE:] = end.astype(BF16)

    @pl.loop(1, EXPERTS)
    def _(o):
        dispatch(o).wait_send()
        give_back(o).wait_send()

    for m in range(3):
        own_side(m, low).wait_send()
    for part in range(2):
        @pl.loop(0, CHUNKS)
        def _(k):
            side(part, k, far).wait_send()

        @pl.when(position[part] == 0)
        def _():
            @pl.loop(0, CHUNKS)
            def _(k):
                cross(part, k).wait_send()

        @pl.when(position[part] < HALF - 1)
        def _():
            @pl.loop(0, CHUNKS)
            def _(k):
                hop(part, k).wait_send()

    arr_copy.wait()


def on_device(tokens, expert_ids, combine, old_gate, old_up, old_down, move_plan):
    vmem = pl.BlockSpec(memory_space=pltpu.VMEM)
    hbm = pl.BlockSpec(memory_space=pl.ANY)
    dma = pltpu.SemaphoreType.DMA
    total = EXPERTS * ROWS
    return pl.pallas_call(
        kernel,
        out_shape=(
            jax.ShapeDtypeStruct((TOK, D), BF16),
            jax.ShapeDtypeStruct((3, MOVE, D), BF16),
        ),
        in_specs=[vmem, vmem, vmem, hbm, hbm, hbm, vmem],
        out_specs=(vmem, hbm),
        scratch_shapes=[
            pltpu.VMEM((3, UNITS, D), BF16),
            pltpu.VMEM((total, WIDE), BF16),
            pltpu.VMEM((total, WIDE), BF16),
            pltpu.VMEM((total, WIDE), BF16),
            pltpu.VMEM((total, WIDE), BF16),
            pltpu.VMEM((BATCH * ROWS, UNITS), BF16),
            pltpu.VMEM((BATCH * ROWS, Q), BF16),
            pltpu.VMEM((3, 512, total), BF16),
            pltpu.VMEM((6, BATCH * ROWS, BATCH * ROWS), BF16),
            pltpu.VMEM((3, MOVE, D), BF16),
            dma((3,)),
            dma((EXPERTS,)),
            dma((EXPERTS,)),
            dma((EXPERTS,)),
            dma((EXPERTS,)),
            dma((2, CHUNKS)),
            dma((2, CHUNKS)),
            dma((2, CHUNKS)),
            dma((2, CHUNKS)),
            dma((2, CHUNKS)),
            dma((3,)),
            dma((3,)),
            dma,
        ],
        compiler_params=pltpu.CompilerParams(
            collective_id=0, has_side_effects=True, vmem_limit_bytes=48 * 1024 * 1024
        ),
        name="moe",
    )(tokens, expert_ids, combine, old_gate, old_up, old_down, move_plan)


def solution(mesh):
    placed = (
        P(("replica", "expert"), None),
        P(("replica", "expert"), None),
        P(("replica", "expert"), None),
        P("expert", None),
        P("expert", None),
        P("expert", None),
        P(),
    )
    return jax.shard_map(
        on_device,
        mesh=mesh,
        in_specs=placed,
        out_specs=(P(("replica", "expert"), None), P("replica", "expert", None)),
        check_vma=False,
    )
```

time: 660 us -> 118 us (0.18)
  the two profiles are of different devices: /device:TPU:8 before, /device:TPU:1 now
where the time goes in v1:
time: 118 us; the launch traced here: 117 us
  Pallas kernels  107 us (91%)
  local copies, waits for them, and re-layouts  8.65 us (7%)
    pallas_call x1, Pallas kernels, on_device(): pl.pallas_call(kernel, out_shape=(jax.ShapeDtypeStruct((TOK, D), BF16), j...  107 us
    unnamed x13, local copies, waits for them, and re-layouts  8.65 us

profile of v1, /device:TPU:1, one launch (start us, length us, event | category | flops | bytes accessed | tf_op | source)
XLA Modules:
  0.0 116.5 jit_solution(9589084278733598417)
XLA Ops:
  0.6 0.8 copy.9.ids
  1.4 0.8 copy.10.comb
  2.2 0.8 copy.11.plan
  3.0 0.0 copy-start
  3.1 1.1 copy-done
  4.2 0.0 copy-start.1
  4.2 1.1 copy-done.1
  5.3 0.0 copy-start.2
  5.3 1.1 copy-done.2
  6.4 0.0 copy-start.3
  6.4 1.0 copy-done.3
  7.5 107.2 %moe.1 = (bf16[128,2048]{1,0:T(8,128)(2,1)S(1)}, bf16[3,96,2048]{2,1,0:T(8,128)(2,1)S(1)}) custom-call(bf16[128,2048]{1,0:T(8,128)(2,1)S(1)} %copy-done.3, s32[128,8]{1,0:T(8,128)S(1)} %copy.9.ids, f32[128,8]{1,0:T(8,128)S(1)} %copy.10.comb, bf16[192,2048]{1,0:T(8,128)(2,1)S(1)} %copy-done, bf16[192,2048]{1,0:T(8,128)(2,1)S(1)} %copy-done.1, ...), custom_call_target="tpu_custom_call" | custom-call | tf_op jit(solution)/shard_map/moe/pallas_call | solution.py:339
  114.7 0.8 copy.14
  115.5 1.0 copy.15
Async XLA Ops:
  3.0 1.1 copy-start
  4.2 1.1 copy-start.1
  5.3 1.1 copy-start.2
  6.4 1.0 copy-start.3

commit v2 on v1

--- a/solution.py
+++ b/solution.py
@@ -20,10 +20,11 @@
 OLD = 192
 UNITS = 4 * OLD
 MOVE = 96
-CHUNKS = 6
+CHUNKS = 18
 PIECE = 3 * OLD // 2 // CHUNKS
 PER = CHUNKS // 3
-BATCH = 16
+SKEW = 3
+BATCH = 8
 NT = (((1,), (1,)), ((), ()))
 
 
@@ -45,9 +46,9 @@
 
 
 def kernel(
-    tok, ids, comb, gate, up, down, plan, mixed, arrived,
-    wts, send, recv, outs, ret, hid, x3, lhs, fold, arr,
-    own_sem, d_send, d_recv, r_send, r_recv, cross_send, hop_send, hop_recv,
+    tokens, expert_ids, combine, gate, up, down, move_plan, mixed, arrived,
+    ids, comb, plan, tok, wts, send, recv, outs, ret, hid, x3, lhs, fold, arr, acc,
+    in_sem, own_sem, d_send, d_recv, r_send, r_recv, cross_send, hop_send, hop_recv,
     side_send, side_recv, twin_send, twin_recv, arr_sem,
 ):
     e = lax.axis_index("expert")
@@ -68,28 +69,33 @@
         there = lax.rem(y + RING + distance, RING)
         return (4 * grp + 2 * lax.div(there, HALF) + core, lax.rem(there, HALF))
 
-    barrier = pltpu.get_barrier_semaphore()
-
-    def greet(device):
-        pl.semaphore_signal(barrier, inc=1, device_id=device, device_id_type=MESH)
-
-    @pl.loop(1, EXPERTS)
-    def _(o):
-        greet(peer(o, 1))
-
-    greet(twin)
-    greet(ring(1))
-    greet(ring(-1))
-
     mats = (gate, up, down)
+    fetched = [
+        pltpu.make_async_copy(source, target, in_sem.at[i])
+        for i, (source, target) in enumerate(((expert_ids, ids), (tokens, tok), (combine, comb), (move_plan, plan)))
+    ]
     own = [
         pltpu.make_async_copy(mats[m], wts.at[m, pl.ds(pl.multiple_of(low * OLD, 16), OLD)], own_sem.at[m])
         for m in range(3)
     ]
-    for copy in own:
+    for copy in fetched + own:
         copy.start()
 
-    ids_t = jnp.transpose(ids[...])
+    barrier = pltpu.get_barrier_semaphore()
+
+    def greet(device):
+        pl.semaphore_signal(barrier, inc=1, device_id=device, device_id_type=MESH)
+
+    @pl.loop(1, EXPERTS)
+    def _(o):
+        greet(peer(o, 1))
+
+    greet(twin)
+    greet(ring(1))
+    greet(ring(-1))
+
+    fetched[0].wait()
+    ids_t = ids[...]
     row = lax.broadcasted_iota(jnp.int32, (128, 128), 0)
     lane = lax.broadcasted_iota(jnp.int32, (128, 128), 1)
     before = one_hot(row < lane)
@@ -111,6 +117,8 @@
         last = [(rank == 3 * (slot - CAP) + b) & (slot >= CAP) for b in range(3)]
         return first, last
 
+    fetched[1].wait()
+
     @pl.loop(0, 4)
     def _(i):
         first, last = places(named(i))
@@ -181,7 +189,8 @@
 
     recv[0:ROWS, :] = send[0:ROWS, :]
 
-    comb_t = jnp.transpose(comb[...])
+    fetched[2].wait()
+    comb_t = comb[...]
 
     @pl.loop(0, 4)
     def _(i):
@@ -214,10 +223,10 @@
             same & ((high_row & 15) >= CAP) & ((low_row & 15) == 3 * ((high_row & 15) - CAP) + b)
         )
 
-    @pl.loop(0, CHUNKS + HALF - 1)
+    @pl.loop(0, CHUNKS + SKEW * (HALF - 1))
     def _(j):
         for part in range(2):
-            k = j - position[part]
+            k = j - SKEW * position[part]
 
             @pl.when((k >= 0) & (k < CHUNKS))
             def _():
@@ -282,7 +291,8 @@
 
     ret[0:ROWS, :] = outs[0:ROWS, :]
 
-    mine = plan[grp, pl.ds(lax.rem(low, 3), 1), :]
+    fetched[3].wait()
+    mine = plan[lax.rem(low, 3), pl.ds(grp, 1), :]
     wanted = lax.broadcasted_iota(jnp.int32, (OLD, MOVE), 0) == mine
     chosen = jnp.transpose(jnp.where(wanted, jnp.where(low < 3, 1.0, 0.0), 0.0)).astype(BF16)
     for m in range(3):
@@ -292,17 +302,28 @@
     arr_copy = pltpu.make_async_copy(arr, arrived, arr_sem)
     arr_copy.start()
 
-    @pl.loop(1, EXPERTS)
-    def _(o):
-        give_back(o).wait_recv()
-
-    end = jnp.zeros((TOK, Q), F32)
-    for b in range(3):
-        columns = slice(b * Q, (b + 1) * Q)
-        sums = dot(lhs[b], ret[:, columns])
-        mixed[:, columns] = (sums[0:128] + sums[128:256]).astype(BF16)
-        end = end + (sums[256:384] + sums[384:512])
-    mixed[:, WIDE:] = end.astype(BF16)
+    acc[...] = jnp.zeros_like(acc)
+
+    @pl.loop(0, EXPERTS // BATCH)
+    def _(i):
+        @pl.loop(0, BATCH)
+        def _(j):
+            o = i * BATCH + j
+
+            @pl.when(o > 0)
+            def _():
+                give_back(o).wait_recv()
+
+        rows = pl.ds(pl.multiple_of(i * n_rows, n_rows), n_rows)
+        end = acc[:, WIDE:]
+        for b in range(3):
+            columns = slice(b * Q, (b + 1) * Q)
+            sums = dot(lhs[b, :, rows], ret[rows, columns])
+            acc[:, columns] = acc[:, columns] + (sums[0:128] + sums[128:256])
+            end = end + (sums[256:384] + sums[384:512])
+        acc[:, WIDE:] = end
+
+    mixed[...] = acc[...].astype(BF16)
 
     @pl.loop(1, EXPERTS)
     def _(o):
@@ -333,18 +354,26 @@
 
 def on_device(tokens, expert_ids, combine, old_gate, old_up, old_down, move_plan):
     vmem = pl.BlockSpec(memory_space=pltpu.VMEM)
-    hbm = pl.BlockSpec(memory_space=pl.ANY)
+    hbm = pl.BlockSpec(memory_space=pltpu.HBM)
     dma = pltpu.SemaphoreType.DMA
     total = EXPERTS * ROWS
+
+    def stay(array):
+        return pltpu.with_memory_space_constraint(array, pltpu.HBM)
+
     return pl.pallas_call(
         kernel,
         out_shape=(
             jax.ShapeDtypeStruct((TOK, D), BF16),
             jax.ShapeDtypeStruct((3, MOVE, D), BF16),
         ),
-        in_specs=[vmem, vmem, vmem, hbm, hbm, hbm, vmem],
+        in_specs=[hbm] * 7,
         out_specs=(vmem, hbm),
         scratch_shapes=[
+            pltpu.VMEM((8, TOK), jnp.int32),
+            pltpu.VMEM((8, TOK), F32),
+            pltpu.VMEM((3, EXPERTS, MOVE), jnp.int32),
+            pltpu.VMEM((TOK, D), BF16),
             pltpu.VMEM((3, UNITS, D), BF16),
             pltpu.VMEM((total, WIDE), BF16),
             pltpu.VMEM((total, WIDE), BF16),
@@ -355,6 +384,8 @@
             pltpu.VMEM((3, 512, total), BF16),
             pltpu.VMEM((6, BATCH * ROWS, BATCH * ROWS), BF16),
             pltpu.VMEM((3, MOVE, D), BF16),
+            pltpu.VMEM((TOK, D), F32),
+            dma((4,)),
             dma((3,)),
             dma((EXPERTS,)),
             dma((EXPERTS,)),
@@ -370,10 +401,13 @@
             dma,
         ],
         compiler_params=pltpu.CompilerParams(
-            collective_id=0, has_side_effects=True, vmem_limit_bytes=48 * 1024 * 1024
+            collective_id=0, has_side_effects=True, vmem_limit_bytes=30 * 1024 * 1024
         ),
         name="moe",
-    )(tokens, expert_ids, combine, old_gate, old_up, old_down, move_plan)
+    )(
+        stay(tokens), stay(expert_ids.T), stay(combine.T), stay(old_gate), stay(old_up), stay(old_down),
+        stay(jnp.transpose(move_plan, (1, 0, 2))),
+    )
 
 
 def solution(mesh):

time: 118 us -> 103 us (0.87); the launches traced: 117 us -> 103 us
  Pallas kernels: 107 us -> 100 us
  local copies, waits for them, and re-layouts: 8.65 us -> 1.81 us
    pallas_call x1, Pallas kernels: 107 us -> 100 us  [on_device(): pl.pallas_call(kernel, out_shape=(jax.ShapeDtypeStruct((TOK, D), BF16), j...]
    unnamed x13 -> x2, local copies, waits for them, and re-layouts: 8.65 us -> 1.81 us
where the time goes in v2:
time: 103 us
  Pallas kernels  100 us (97%)
  local copies, waits for them, and re-layouts  1.81 us (2%)
    pallas_call x1, Pallas kernels, on_device(): pl.pallas_call(kernel, out_shape=(jax.ShapeDtypeStruct((TOK, D), BF16), j...  100 us

profile of v2, /device:TPU:1, one launch (start us, length us, event | category | flops | bytes accessed | tf_op | source)
XLA Modules:
  0.0 102.8 jit_solution(8138522474032622526)
XLA Ops:
  0.6 100.4 %moe.1 = (bf16[128,2048]{1,0:T(8,128)(2,1)S(1)}, bf16[3,96,2048]{2,1,0:T(8,128)(2,1)S(1)}) custom-call(bf16[128,2048]{1,0:T(8,128)(2,1)} %tokens.1, s32[8,128]{1,0:T(8,128)} %bitcast.4, f32[8,128]{1,0:T(8,128)} %bitcast.5, bf16[192,2048]{1,0:T(8,128)(2,1)} %gate.1, bf16[192,2048]{1,0:T(8,128)(2,1)} %up.1, bf16[192,2048]{1,0:T(8,128)(2,1)} %down.1, ...), custom_call_target="tpu_custom_call" | custom-call | tf_op jit(solution)/shard_map/moe/pallas_call | solution.py:364
  101.0 0.8 copy.11
  101.8 1.0 copy.12

commit v3 on v2

--- a/solution.py
+++ b/solution.py
@@ -20,9 +20,13 @@
 OLD = 192
 UNITS = 4 * OLD
 MOVE = 96
-CHUNKS = 18
-PIECE = 3 * OLD // 2 // CHUNKS
-PER = CHUNKS // 3
+PIECES = 18
+PIECE = 16
+PER = OLD // 2 // PIECE
+TAIL = 3
+FULL = PIECES - TAIL
+LONG = PIECES + TAIL
+EARLY = 2 * PER
 SKEW = 3
 BATCH = 8
 NT = (((1,), (1,)), ((), ()))
@@ -128,89 +132,6 @@
             part = dot(first, tok[:, b * Q : (b + 1) * Q]) + dot(one_hot(last[b]), tok[:, WIDE:])
             send[rows, b * Q : (b + 1) * Q] = part.astype(BF16)
 
-    pl.semaphore_wait(barrier, EXPERTS + 2)
-
-    def piece(owner, part, k):
-        start = owner * OLD + part * (OLD // 2) + lax.rem(k, PER) * PIECE
-        return wts.at[lax.div(k, PER), pl.ds(pl.multiple_of(start, 16), PIECE)]
-
-    def passing(ref, sender, receiver, device):
-        return pltpu.make_async_remote_copy(
-            src_ref=ref, dst_ref=ref, send_sem=sender, recv_sem=receiver, device_id=device, device_id_type=MESH
-        )
-
-    position = (half * rep + (1 - half) * (HALF - 1 - rep), half * (HALF - 1 - rep) + (1 - half) * rep)
-    ahead = (ring(step), ring(-step))
-    behind = (ring(-step), ring(step))
-    far = lax.rem(low + 2, 4)
-
-    def cross(part, k):
-        return passing(piece(low, part, k), cross_send.at[part, k], hop_recv.at[part, k], behind[part])
-
-    def hop(part, k):
-        return passing(piece(far, part, k), hop_send.at[part, k], hop_recv.at[part, k], ahead[part])
-
-    def side(part, k, owner):
-        return passing(piece(owner, part, k), side_send.at[part, k], side_recv.at[part, k], twin)
-
-    def own_side(m, owner):
-        ref = wts.at[m, pl.ds(pl.multiple_of(owner * OLD, 16), OLD)]
-        return passing(ref, twin_send.at[m], twin_recv.at[m], twin)
-
-    for copy in own:
-        copy.wait()
-
-    for part in range(2):
-        @pl.when(position[part] == 0)
-        def _():
-            @pl.loop(0, CHUNKS)
-            def _(k):
-                cross(part, k).start()
-
-    def parcel(source, target, o, sender, receiver, device):
-        rows = pl.ds(pl.multiple_of(o * ROWS, ROWS), ROWS)
-        return pltpu.make_async_remote_copy(
-            src_ref=source.at[rows], dst_ref=target.at[rows], send_sem=sender.at[o], recv_sem=receiver.at[o],
-            device_id=device, device_id_type=MESH,
-        )
-
-    def dispatch(o):
-        return parcel(send, recv, o, d_send, d_recv, peer(o, 1))
-
-    def give_back(o):
-        return parcel(outs, ret, o, r_send, r_recv, peer(o, -1))
-
-    @pl.loop(1, EXPERTS)
-    def _(o):
-        dispatch(o).start()
-
-    for m in range(3):
-        own_side(m, low).start()
-
-    recv[0:ROWS, :] = send[0:ROWS, :]
-
-    fetched[2].wait()
-    comb_t = comb[...]
-
-    @pl.loop(0, 4)
-    def _(i):
-        hits = named(i)
-        first, last = places(hits)
-        weight = jnp.zeros((128, 128), F32)
-        for k in range(8):
-            weight = weight + jnp.where(hits[k], comb_t[k : k + 1, :], 0.0)
-        columns = pl.ds(pl.multiple_of(i * 128, 128), 128)
-
-        def store(b, at, chosen):
-            value = jnp.transpose(jnp.where(chosen, weight, 0.0))
-            high = value.astype(BF16)
-            lhs[b, at : at + 128, columns] = high
-            lhs[b, at + 128 : at + 256, columns] = (value - high.astype(F32)).astype(BF16)
-
-        for b in range(3):
-            store(b, 0, first)
-            store(b, 256, last[b])
-
     n_rows = BATCH * ROWS
     low_row = lax.broadcasted_iota(jnp.int32, (n_rows, n_rows), 0)
     high_row = lax.broadcasted_iota(jnp.int32, (n_rows, n_rows), 1)
@@ -223,29 +144,115 @@
             same & ((high_row & 15) >= CAP) & ((low_row & 15) == 3 * ((high_row & 15) - CAP) + b)
         )
 
-    @pl.loop(0, CHUNKS + SKEW * (HALF - 1))
+    pl.semaphore_wait(barrier, EXPERTS + 2)
+
+    def piece(owner, d, q):
+        tail = q >= FULL
+        extra = lax.max(q - FULL, 0)
+        part = jnp.where(tail, lax.rem(extra, 2), d)
+        k = jnp.where(tail, FULL + lax.div(extra, 2), q)
+        start = owner * OLD + part * (OLD // 2) + lax.rem(k, PER) * PIECE
+        return wts.at[lax.div(k, PER), pl.ds(pl.multiple_of(start, PIECE), PIECE)]
+
+    def passing(ref, sender, receiver, device):
+        return pltpu.make_async_remote_copy(
+            src_ref=ref, dst_ref=ref, send_sem=sender, recv_sem=receiver, device_id=device, device_id_type=MESH
+        )
+
+    position = (half * rep + (1 - half) * (HALF - 1 - rep), half * (HALF - 1 - rep) + (1 - half) * rep)
+    ahead = (ring(step), ring(-step))
+    behind = (ring(-step), ring(step))
+    far = lax.rem(low + 2, 4)
+
+    def cross(d, q):
+        return passing(piece(low, d, q), cross_send.at[d, q], hop_recv.at[d, q], behind[d])
+
+    def hop(d, q):
+        return passing(piece(far, d, q), hop_send.at[d, q], hop_recv.at[d, q], ahead[d])
+
+    def side(d, q, owner):
+        return passing(piece(owner, d, q), side_send.at[d, q], side_recv.at[d, q], twin)
+
+    def reaches(d, q):
+        return (q >= 0) & (q < LONG) & ((q < FULL) | (position[d] < 2))
+
+    def forwards(d, q):
+        return (position[d] == 0) | ((position[d] < HALF - 1) & (q < FULL))
+
+    def own_side(m, owner):
+        ref = wts.at[m, pl.ds(pl.multiple_of(owner * OLD, 16), OLD)]
+        return passing(ref, twin_send.at[m], twin_recv.at[m], twin)
+
+    for copy in own:
+        copy.wait()
+
+    for d in range(2):
+        @pl.when(position[d] == 0)
+        def _():
+            @pl.loop(0, LONG)
+            def _(q):
+                cross(d, q).start()
+
+    def parcel(source, target, o, sender, receiver, device):
+        rows = pl.ds(pl.multiple_of(o * ROWS, ROWS), ROWS)
+        return pltpu.make_async_remote_copy(
+            src_ref=source.at[rows], dst_ref=target.at[rows], send_sem=sender.at[o], recv_sem=receiver.at[o],
+            device_id=device, device_id_type=MESH,
+        )
+
+    def dispatch(o):
+        return parcel(send, recv, o, d_send, d_recv, peer(o, 1))
+
+    def give_back(o):
+        return parcel(outs, ret, o, r_send, r_recv, peer(o, -1))
+
+    @pl.loop(1, BATCH)
+    def _(o):
+        dispatch(o).start()
+
+    for m in range(3):
+        own_side(m, low).start()
+
+    recv[0:ROWS, :] = send[0:ROWS, :]
+
+    @pl.loop(0, FULL + SKEW * (HALF - 1))
     def _(j):
-        for part in range(2):
-            k = j - SKEW * position[part]
-
-            @pl.when((k >= 0) & (k < CHUNKS))
-            def _():
-                hop(part, k).wait_recv()
-
-                @pl.when(position[part] < HALF - 1)
+        for d in range(2):
+            q = j - SKEW * position[d]
+
+            @pl.when(reaches(d, q))
+            def _():
+                hop(d, q).wait_recv()
+
+                @pl.when(forwards(d, q))
                 def _():
-                    hop(part, k).start()
-
-                side(part, k, far).start()
-
-    for m in range(3):
-        own_side(m, lax.rem(low + 1, 2) + 2 * half).wait_recv()
-
-    @pl.loop(0, CHUNKS)
-    def _(k):
-        for part in range(2):
-            side(part, k, lax.rem(far + 1, 2) + 2 * (1 - half)).wait_recv()
-
+                    hop(d, q).start()
+
+                side(d, q, far).start()
+
+        @pl.when(j < (EXPERTS - BATCH) // 4)
+        def _():
+            for o in range(4):
+                dispatch(BATCH + 4 * j + o).start()
+
+    twin_low, twin_far = lax.rem(low + 1, 2) + 2 * half, lax.rem(far + 1, 2) + 2 * (1 - half)
+
+    def side_waits(first, last):
+        @pl.loop(first, last)
+        def _(q):
+            for d in range(2):
+                @pl.when(reaches(d, q))
+                def _():
+                    side(d, q, twin_far).wait_recv()
+
+    def batch_rows(i):
+        return pl.ds(pl.multiple_of(i * n_rows, n_rows), n_rows)
+
+    for m in range(2):
+        own_side(m, twin_low).wait_recv()
+    side_waits(0, EARLY)
+
+    tiles = UNITS // 256
     out_slot = lax.broadcasted_iota(jnp.int32, (n_rows, Q), 0) & 15
 
     @pl.loop(0, EXPERTS // BATCH)
@@ -258,13 +265,13 @@
             def _():
                 dispatch(o).wait_recv()
 
-        rows = pl.ds(pl.multiple_of(i * n_rows, n_rows), n_rows)
+        rows = batch_rows(i)
         tail = dot(fold[3], recv[rows, 0:Q])
         for b in range(1, 3):
             tail = tail + dot(fold[3 + b], recv[rows, b * Q : (b + 1) * Q])
         x3[...] = tail.astype(BF16)
 
-        @pl.loop(0, UNITS // 256)
+        @pl.loop(0, tiles)
         def _(n):
             units = pl.ds(pl.multiple_of(n * 256, 256), 256)
 
@@ -274,6 +281,11 @@
             gate_value = project(0)
             hidden = gate_value / (1.0 + jnp.exp(-gate_value)) * project(1)
             hid[:, units] = hidden.astype(BF16)
+
+        @pl.when(i == 0)
+        def _():
+            own_side(2, twin_low).wait_recv()
+            side_waits(EARLY, LONG)
 
         last = dot(hid[...], wts[2, :, WIDE:]).astype(BF16)
         for b in range(3):
@@ -290,6 +302,28 @@
                 give_back(o).start()
 
     ret[0:ROWS, :] = outs[0:ROWS, :]
+
+    fetched[2].wait()
+    comb_t = comb[...]
+
+    @pl.loop(0, 4)
+    def _(i):
+        hits = named(i)
+        first, last = places(hits)
+        weight = jnp.zeros((128, 128), F32)
+        for k in range(8):
+            weight = weight + jnp.where(hits[k], comb_t[k : k + 1, :], 0.0)
+        columns = pl.ds(pl.multiple_of(i * 128, 128), 128)
+
+        def store(b, at, chosen):
+            value = jnp.transpose(jnp.where(chosen, weight, 0.0))
+            high = value.astype(BF16)
+            lhs[b, at : at + 128, columns] = high
+            lhs[b, at + 128 : at + 256, columns] = (value - high.astype(F32)).astype(BF16)
+
+        for b in range(3):
+            store(b, 0, first)
+            store(b, 256, last[b])
 
     fetched[3].wait()
     mine = plan[lax.rem(low, 3), pl.ds(grp, 1), :]
@@ -302,6 +336,28 @@
     arr_copy = pltpu.make_async_copy(arr, arrived, arr_sem)
     arr_copy.start()
 
+    @pl.loop(1, EXPERTS)
+    def _(o):
+        dispatch(o).wait_send()
+
+    for m in range(3):
+        own_side(m, low).wait_send()
+
+    @pl.loop(0, LONG)
+    def _(q):
+        for d in range(2):
+            @pl.when(reaches(d, q))
+            def _():
+                side(d, q, far).wait_send()
+
+            @pl.when(reaches(d, q) & forwards(d, q))
+            def _():
+                hop(d, q).wait_send()
+
+            @pl.when(position[d] == 0)
+            def _():
+                cross(d, q).wait_send()
+
     acc[...] = jnp.zeros_like(acc)
 
     @pl.loop(0, EXPERTS // BATCH)
@@ -313,6 +369,7 @@
             @pl.when(o > 0)
             def _():
                 give_back(o).wait_recv()
+                give_back(o).wait_send()
 
         rows = pl.ds(pl.multiple_of(i * n_rows, n_rows), n_rows)
         end = acc[:, WIDE:]
@@ -324,30 +381,6 @@
         acc[:, WIDE:] = end
 
     mixed[...] = acc[...].astype(BF16)
-
-    @pl.loop(1, EXPERTS)
-    def _(o):
-        dispatch(o).wait_send()
-        give_back(o).wait_send()
-
-    for m in range(3):
-        own_side(m, low).wait_send()
-    for part in range(2):
-        @pl.loop(0, CHUNKS)
-        def _(k):
-            side(part, k, far).wait_send()
-
-        @pl.when(position[part] == 0)
-        def _():
-            @pl.loop(0, CHUNKS)
-            def _(k):
-                cross(part, k).wait_send()
-
-        @pl.when(position[part] < HALF - 1)
-        def _():
-            @pl.loop(0, CHUNKS)
-            def _(k):
-                hop(part, k).wait_send()
 
     arr_copy.wait()
 
@@ -391,11 +424,11 @@
             dma((EXPERTS,)),
             dma((EXPERTS,)),
             dma((EXPERTS,)),
-            dma((2, CHUNKS)),
-            dma((2, CHUNKS)),
-            dma((2, CHUNKS)),
-            dma((2, CHUNKS)),
-            dma((2, CHUNKS)),
+            dma((2, LONG)),
+            dma((2, LONG)),
+            dma((2, LONG)),
+            dma((2, LONG)),
+            dma((2, LONG)),
             dma((3,)),
             dma((3,)),
             dma,

time: 103 us -> 96.5 us (0.937)
  the two profiles are of different devices: /device:TPU:1 before, /device:TPU:16 now
where the time goes in v3:
time: 96.5 us; the launch traced here: 96.3 us
  Pallas kernels  93.9 us (97%)
  local copies, waits for them, and re-layouts  1.81 us (2%)
    pallas_call x1, Pallas kernels, on_device(): pl.pallas_call(kernel, out_shape=(jax.ShapeDtypeStruct((TOK, D), BF16), j...  93.9 us

profile of v3, /device:TPU:16, one launch (start us, length us, event | category | flops | bytes accessed | tf_op | source)
XLA Modules:
  0.0 96.3 jit_solution(1289561651274571201)
XLA Ops:
  0.6 93.9 %moe.1 = (bf16[128,2048]{1,0:T(8,128)(2,1)S(1)}, bf16[3,96,2048]{2,1,0:T(8,128)(2,1)S(1)}) custom-call(bf16[128,2048]{1,0:T(8,128)(2,1)} %tokens.1, s32[8,128]{1,0:T(8,128)} %bitcast.4, f32[8,128]{1,0:T(8,128)} %bitcast.5, bf16[192,2048]{1,0:T(8,128)(2,1)} %gate.1, bf16[192,2048]{1,0:T(8,128)(2,1)} %up.1, bf16[192,2048]{1,0:T(8,128)(2,1)} %down.1, ...), custom_call_target="tpu_custom_call" | custom-call | tf_op jit(solution)/shard_map/moe/pallas_call | solution.py:397
  94.5 0.8 copy.11
  95.3 1.0 %copy.12 = bf16[3,96,2048]{2,1,0:T(8,128)(2,1)} copy(bf16[3,96,2048]{2,1,0:T(8,128)(2,1)S(1)} %get-tuple-element.5) | data formatting | bytes 2359296

commit v4 on v3

--- a/solution.py
+++ b/solution.py
@@ -46,14 +46,14 @@
 
 def z_offset(k):
     odd = lax.rem(k, 2)
-    return odd * lax.div(k + 1, 2) + (1 - odd) * lax.rem(Z - lax.div(k, 2), Z)
+    return odd * (HALF + lax.div(k, 2)) + (1 - odd) * lax.rem(HALF - lax.div(k, 2), HALF)
 
 
 def kernel(
     tokens, expert_ids, combine, gate, up, down, move_plan, mixed, arrived,
     ids, comb, plan, tok, wts, send, recv, outs, ret, hid, x3, lhs, fold, arr, acc,
     in_sem, own_sem, d_send, d_recv, r_send, r_recv, cross_send, hop_send, hop_recv,
-    side_send, side_recv, twin_send, twin_recv, arr_sem,
+    side_send, side_recv, arr_sem,
 ):
     e = lax.axis_index("expert")
     rep = lax.axis_index("replica")
@@ -107,7 +107,7 @@
 
     def named(i):
         k = row >> 4
-        oz = jnp.where((k & 1) == 1, (k + 1) >> 1, (8 - (k >> 1)) & 7)
+        oz = jnp.where((k & 1) == 1, HALF + (k >> 1), (HALF - (k >> 1)) & 3)
         g = ((gx + i) & 3) * Z + ((gz + oz) & 7)
         return [ids_t[k : k + 1, :] == g for k in range(8)]
 
@@ -123,14 +123,15 @@
 
     fetched[1].wait()
 
-    @pl.loop(0, 4)
-    def _(i):
+    def fill(i):
         first, last = places(named(i))
         rows = pl.ds(pl.multiple_of(i * 128, 128), 128)
         first = one_hot(first)
         for b in range(3):
             part = dot(first, tok[:, b * Q : (b + 1) * Q]) + dot(one_hot(last[b]), tok[:, WIDE:])
             send[rows, b * Q : (b + 1) * Q] = part.astype(BF16)
+
+    fill(0)
 
     n_rows = BATCH * ROWS
     low_row = lax.broadcasted_iota(jnp.int32, (n_rows, n_rows), 0)
@@ -146,6 +147,9 @@
 
     pl.semaphore_wait(barrier, EXPERTS + 2)
 
+    def batch_rows(i):
+        return pl.ds(pl.multiple_of(i * n_rows, n_rows), n_rows)
+
     def piece(owner, d, q):
         tail = q >= FULL
         extra = lax.max(q - FULL, 0)
@@ -165,13 +169,13 @@
     far = lax.rem(low + 2, 4)
 
     def cross(d, q):
-        return passing(piece(low, d, q), cross_send.at[d, q], hop_recv.at[d, q], behind[d])
+        return passing(piece(low, d, q), cross_send.at[d], hop_recv.at[d, q], behind[d])
 
     def hop(d, q):
-        return passing(piece(far, d, q), hop_send.at[d, q], hop_recv.at[d, q], ahead[d])
+        return passing(piece(far, d, q), hop_send.at[d], hop_recv.at[d, q], ahead[d])
 
     def side(d, q, owner):
-        return passing(piece(owner, d, q), side_send.at[d, q], side_recv.at[d, q], twin)
+        return passing(piece(owner, d, q), side_send, side_recv.at[lax.div(q, EARLY)], twin)
 
     def reaches(d, q):
         return (q >= 0) & (q < LONG) & ((q < FULL) | (position[d] < 2))
@@ -181,7 +185,7 @@
 
     def own_side(m, owner):
         ref = wts.at[m, pl.ds(pl.multiple_of(owner * OLD, 16), OLD)]
-        return passing(ref, twin_send.at[m], twin_recv.at[m], twin)
+        return passing(ref, side_send, side_recv.at[m // 2], twin)
 
     for copy in own:
         copy.wait()
@@ -196,7 +200,7 @@
     def parcel(source, target, o, sender, receiver, device):
         rows = pl.ds(pl.multiple_of(o * ROWS, ROWS), ROWS)
         return pltpu.make_async_remote_copy(
-            src_ref=source.at[rows], dst_ref=target.at[rows], send_sem=sender.at[o], recv_sem=receiver.at[o],
+            src_ref=source.at[rows], dst_ref=target.at[rows], send_sem=sender, recv_sem=receiver.at[lax.div(o, BATCH)],
             device_id=device, device_id_type=MESH,
         )
 
@@ -205,6 +209,18 @@
 
     def give_back(o):
         return parcel(outs, ret, o, r_send, r_recv, peer(o, -1))
+
+    def kept(source, target, receiver):
+        return pltpu.make_async_copy(source.at[0:ROWS], target.at[0:ROWS], receiver.at[0])
+
+    def landed(ref, receiver, i):
+        rows = batch_rows(i)
+        passing(ref.at[rows], d_send, receiver.at[i], twin).wait_recv()
+
+    def left(ref, sender):
+        passing(ref, sender, d_recv.at[0], twin).wait_send()
+
+    kept(send, recv, d_recv).start()
 
     @pl.loop(1, BATCH)
     def _(o):
@@ -213,7 +229,9 @@
     for m in range(3):
         own_side(m, low).start()
 
-    recv[0:ROWS, :] = send[0:ROWS, :]
+    @pl.loop(1, EXPERTS // BATCH)
+    def _(i):
+        fill(i)
 
     @pl.loop(0, FULL + SKEW * (HALF - 1))
     def _(j):
@@ -235,36 +253,17 @@
             for o in range(4):
                 dispatch(BATCH + 4 * j + o).start()
 
-    twin_low, twin_far = lax.rem(low + 1, 2) + 2 * half, lax.rem(far + 1, 2) + 2 * (1 - half)
-
-    def side_waits(first, last):
-        @pl.loop(first, last)
-        def _(q):
-            for d in range(2):
-                @pl.when(reaches(d, q))
-                def _():
-                    side(d, q, twin_far).wait_recv()
-
-    def batch_rows(i):
-        return pl.ds(pl.multiple_of(i * n_rows, n_rows), n_rows)
-
-    for m in range(2):
-        own_side(m, twin_low).wait_recv()
-    side_waits(0, EARLY)
-
+    def side_landed(i):
+        rows = wts.at[0] if i == 0 else wts.at[0, 0 : UNITS // 2]
+        passing(rows, side_send, side_recv.at[i], twin).wait_recv()
+
+    side_landed(0)
     tiles = UNITS // 256
     out_slot = lax.broadcasted_iota(jnp.int32, (n_rows, Q), 0) & 15
 
     @pl.loop(0, EXPERTS // BATCH)
     def _(i):
-        @pl.loop(0, BATCH)
-        def _(j):
-            o = i * BATCH + j
-
-            @pl.when(o > 0)
-            def _():
-                dispatch(o).wait_recv()
-
+        landed(recv, d_recv, i)
         rows = batch_rows(i)
         tail = dot(fold[3], recv[rows, 0:Q])
         for b in range(1, 3):
@@ -284,8 +283,7 @@
 
         @pl.when(i == 0)
         def _():
-            own_side(2, twin_low).wait_recv()
-            side_waits(EARLY, LONG)
+            side_landed(1)
 
         last = dot(hid[...], wts[2, :, WIDE:]).astype(BF16)
         for b in range(3):
@@ -301,7 +299,7 @@
             def _():
                 give_back(o).start()
 
-    ret[0:ROWS, :] = outs[0:ROWS, :]
+    kept(outs, ret, r_recv).start()
 
     fetched[2].wait()
     comb_t = comb[...]
@@ -336,52 +334,45 @@
     arr_copy = pltpu.make_async_copy(arr, arrived, arr_sem)
     arr_copy.start()
 
-    @pl.loop(1, EXPERTS)
-    def _(o):
-        dispatch(o).wait_send()
-
-    for m in range(3):
-        own_side(m, low).wait_send()
-
-    @pl.loop(0, LONG)
-    def _(q):
-        for d in range(2):
-            @pl.when(reaches(d, q))
-            def _():
-                side(d, q, far).wait_send()
-
-            @pl.when(reaches(d, q) & forwards(d, q))
-            def _():
-                hop(d, q).wait_send()
-
-            @pl.when(position[d] == 0)
-            def _():
-                cross(d, q).wait_send()
+    left(send.at[0 : (EXPERTS - 1) * ROWS], d_send)
+    left(wts.at[0:2, 0 : 3 * OLD], side_send)
+    for d in range(2):
+        @pl.when(position[d] == 0)
+        def _():
+            left(wts.at[0, 0 : LONG * PIECE], cross_send.at[d])
+            left(wts.at[0, 0 : LONG * PIECE], hop_send.at[d])
+
+        @pl.when((position[d] == 1) | (position[d] == 2))
+        def _():
+            left(wts.at[0, 0 : FULL * PIECE], hop_send.at[d])
+
+    def sums(i, b):
+        found = dot(lhs[b, :, batch_rows(i)], ret[batch_rows(i), b * Q : (b + 1) * Q])
+        return found[0:128] + found[128:256], found[256:384] + found[384:512]
 
     acc[...] = jnp.zeros_like(acc)
 
-    @pl.loop(0, EXPERTS // BATCH)
+    @pl.loop(0, EXPERTS // BATCH - 1)
     def _(i):
-        @pl.loop(0, BATCH)
-        def _(j):
-            o = i * BATCH + j
-
-            @pl.when(o > 0)
-            def _():
-                give_back(o).wait_recv()
-                give_back(o).wait_send()
-
-        rows = pl.ds(pl.multiple_of(i * n_rows, n_rows), n_rows)
+        landed(ret, r_recv, i)
         end = acc[:, WIDE:]
         for b in range(3):
             columns = slice(b * Q, (b + 1) * Q)
-            sums = dot(lhs[b, :, rows], ret[rows, columns])
-            acc[:, columns] = acc[:, columns] + (sums[0:128] + sums[128:256])
-            end = end + (sums[256:384] + sums[384:512])
+            wide, more = sums(i, b)
+            acc[:, columns] = acc[:, columns] + wide
+            end = end + more
         acc[:, WIDE:] = end
 
-    mixed[...] = acc[...].astype(BF16)
-
+    final = EXPERTS // BATCH - 1
+    landed(ret, r_recv, final)
+    end = acc[:, WIDE:]
+    for b in range(3):
+        columns = slice(b * Q, (b + 1) * Q)
+        wide, more = sums(final, b)
+        mixed[:, columns] = (acc[:, columns] + wide).astype(BF16)
+        end = end + more
+    mixed[:, WIDE:] = end.astype(BF16)
+    left(outs.at[0 : (EXPERTS - 1) * ROWS], r_send)
     arr_copy.wait()
 
 
@@ -420,17 +411,15 @@
             pltpu.VMEM((TOK, D), F32),
             dma((4,)),
             dma((3,)),
-            dma((EXPERTS,)),
-            dma((EXPERTS,)),
-            dma((EXPERTS,)),
-            dma((EXPERTS,)),
+            dma,
+            dma((EXPERTS // BATCH,)),
+            dma,
+            dma((EXPERTS // BATCH,)),
+            dma((2,)),
+            dma((2,)),
             dma((2, LONG)),
-            dma((2, LONG)),
-            dma((2, LONG)),
-            dma((2, LONG)),
-            dma((2, LONG)),
-            dma((3,)),
-            dma((3,)),
+            dma,
+            dma((2,)),
             dma,
         ],
         compiler_params=pltpu.CompilerParams(

time: 96.5 us -> 93 us (0.964)
  the two profiles are of different devices: /device:TPU:16 before, /device:TPU:1 now
where the time goes in v4:
time: 93 us; the launch traced here: 91.3 us
  Pallas kernels  88.8 us (95%)
  local copies, waits for them, and re-layouts  1.81 us (2%)
    pallas_call x1, Pallas kernels, on_device(): pl.pallas_call(kernel, out_shape=(jax.ShapeDtypeStruct((TOK, D), BF16), j...  88.8 us

profile of v4, /device:TPU:1, one launch (start us, length us, event | category | flops | bytes accessed | tf_op | source)
XLA Modules:
  0.0 91.3 jit_solution(10474215733882901606)
XLA Ops:
  0.6 88.8 %moe.1 = (bf16[128,2048]{1,0:T(8,128)(2,1)S(1)}, bf16[3,96,2048]{2,1,0:T(8,128)(2,1)S(1)}) custom-call(bf16[128,2048]{1,0:T(8,128)(2,1)} %tokens.1, s32[8,128]{1,0:T(8,128)} %bitcast.4, f32[8,128]{1,0:T(8,128)} %bitcast.5, bf16[192,2048]{1,0:T(8,128)(2,1)} %gate.1, bf16[192,2048]{1,0:T(8,128)(2,1)} %up.1, bf16[192,2048]{1,0:T(8,128)(2,1)} %down.1, ...), custom_call_target="tpu_custom_call" | custom-call | tf_op jit(solution)/shard_map/moe/pallas_call | solution.py:388
  89.5 0.8 copy.11
  90.3 1.0 %copy.12 = bf16[3,96,2048]{2,1,0:T(8,128)(2,1)} copy(bf16[3,96,2048]{2,1,0:T(8,128)(2,1)S(1)} %get-tuple-element.5) | data formatting | bytes 2359296

commit v5 on v4

--- a/solution.py
+++ b/solution.py
@@ -28,6 +28,7 @@
 LONG = PIECES + TAIL
 EARLY = 2 * PER
 SKEW = 3
+PACE = 5
 BATCH = 8
 NT = (((1,), (1,)), ((), ()))
 
@@ -82,7 +83,7 @@
         pltpu.make_async_copy(mats[m], wts.at[m, pl.ds(pl.multiple_of(low * OLD, 16), OLD)], own_sem.at[m])
         for m in range(3)
     ]
-    for copy in fetched + own:
+    for copy in own + fetched:
         copy.start()
 
     barrier = pltpu.get_barrier_semaphore()
@@ -97,6 +98,66 @@
     greet(twin)
     greet(ring(1))
     greet(ring(-1))
+
+    pl.semaphore_wait(barrier, EXPERTS + 2)
+
+    n_rows = BATCH * ROWS
+
+    def batch_rows(i):
+        return pl.ds(pl.multiple_of(i * n_rows, n_rows), n_rows)
+
+    def piece(owner, d, q):
+        tail = q >= FULL
+        extra = lax.max(q - FULL, 0)
+        part = jnp.where(tail, lax.rem(extra, 2), d)
+        k = jnp.where(tail, FULL + lax.div(extra, 2), q)
+        start = owner * OLD + part * (OLD // 2) + lax.rem(k, PER) * PIECE
+        return wts.at[lax.div(k, PER), pl.ds(pl.multiple_of(start, PIECE), PIECE)]
+
+    def passing(ref, sender, receiver, device):
+        return pltpu.make_async_remote_copy(
+            src_ref=ref, dst_ref=ref, send_sem=sender, recv_sem=receiver, device_id=device, device_id_type=MESH
+        )
+
+    place = half * rep + (1 - half) * (HALF - 1 - rep)
+    early = lax.div(place, 2)
+    position = ((1 - early) * place + early * (HALF - 1 - place), early * place + (1 - early) * (HALF - 1 - place))
+    way = step * (1 - 2 * early)
+    direction = (early, 1 - early)
+    ahead = (ring(way), ring(-way))
+    behind = (ring(-way), ring(way))
+    far = lax.rem(low + 2, 4)
+
+    def cross(d, q):
+        return passing(piece(low, direction[d], q), cross_send, hop_recv.at[direction[d], q], behind[d])
+
+    def hop(d, q):
+        return passing(piece(far, direction[d], q), hop_send.at[d], hop_recv.at[direction[d], q], ahead[d])
+
+    def side(d, q, owner):
+        return passing(piece(owner, direction[d], q), side_send, side_recv.at[lax.div(q, EARLY)], twin)
+
+    def reaches(d, q):
+        return (q >= 0) & (q < (LONG if d == 0 else FULL))
+
+    def forwards(d, q):
+        return ((position[0] == 0) | (q < FULL)) if d == 0 else (position[1] == 2)
+
+    def own_side(m, owner):
+        ref = wts.at[m, pl.ds(pl.multiple_of(owner * OLD, 16), OLD)]
+        return passing(ref, side_send, side_recv.at[m // 2], twin)
+
+    for copy in own:
+        copy.wait()
+
+    def cross_from(first, last):
+        @pl.when(position[0] == 0)
+        def _():
+            @pl.loop(first, last)
+            def _(q):
+                cross(0, q).start()
+
+    cross_from(0, 4)
 
     fetched[0].wait()
     ids_t = ids[...]
@@ -133,7 +194,39 @@
 
     fill(0)
 
-    n_rows = BATCH * ROWS
+    def parcel(source, target, o, sender, receiver, device):
+        rows = pl.ds(pl.multiple_of(o * ROWS, ROWS), ROWS)
+        return pltpu.make_async_remote_copy(
+            src_ref=source.at[rows], dst_ref=target.at[rows], send_sem=sender, recv_sem=receiver.at[lax.div(o, BATCH)],
+            device_id=device, device_id_type=MESH,
+        )
+
+    def dispatch(o):
+        return parcel(send, recv, o, d_send, d_recv, peer(o, 1))
+
+    def give_back(o):
+        return parcel(outs, ret, o, r_send, r_recv, peer(o, -1))
+
+    def kept(source, target, receiver):
+        return pltpu.make_async_copy(source.at[0:ROWS], target.at[0:ROWS], receiver.at[0])
+
+    def landed(ref, receiver, i):
+        rows = batch_rows(i)
+        passing(ref.at[rows], d_send, receiver.at[i], twin).wait_recv()
+
+    def left(ref, sender):
+        passing(ref, sender, d_recv.at[0], twin).wait_send()
+
+    kept(send, recv, d_recv).start()
+
+    @pl.loop(1, BATCH)
+    def _(o):
+        dispatch(o).start()
+
+    cross_from(4, LONG)
+    for m in range(3):
+        own_side(m, low).start()
+
     low_row = lax.broadcasted_iota(jnp.int32, (n_rows, n_rows), 0)
     high_row = lax.broadcasted_iota(jnp.int32, (n_rows, n_rows), 1)
     same = (low_row >> 4) == (high_row >> 4)
@@ -145,95 +238,7 @@
             same & ((high_row & 15) >= CAP) & ((low_row & 15) == 3 * ((high_row & 15) - CAP) + b)
         )
 
-    pl.semaphore_wait(barrier, EXPERTS + 2)
-
-    def batch_rows(i):
-        return pl.ds(pl.multiple_of(i * n_rows, n_rows), n_rows)
-
-    def piece(owner, d, q):
-        tail = q >= FULL
-        extra = lax.max(q - FULL, 0)
-        part = jnp.where(tail, lax.rem(extra, 2), d)
-        k = jnp.where(tail, FULL + lax.div(extra, 2), q)
-        start = owner * OLD + part * (OLD // 2) + lax.rem(k, PER) * PIECE
-        return wts.at[lax.div(k, PER), pl.ds(pl.multiple_of(start, PIECE), PIECE)]
-
-    def passing(ref, sender, receiver, device):
-        return pltpu.make_async_remote_copy(
-            src_ref=ref, dst_ref=ref, send_sem=sender, recv_sem=receiver, device_id=device, device_id_type=MESH
-        )
-
-    position = (half * rep + (1 - half) * (HALF - 1 - rep), half * (HALF - 1 - rep) + (1 - half) * rep)
-    ahead = (ring(step), ring(-step))
-    behind = (ring(-step), ring(step))
-    far = lax.rem(low + 2, 4)
-
-    def cross(d, q):
-        return passing(piece(low, d, q), cross_send.at[d], hop_recv.at[d, q], behind[d])
-
-    def hop(d, q):
-        return passing(piece(far, d, q), hop_send.at[d], hop_recv.at[d, q], ahead[d])
-
-    def side(d, q, owner):
-        return passing(piece(owner, d, q), side_send, side_recv.at[lax.div(q, EARLY)], twin)
-
-    def reaches(d, q):
-        return (q >= 0) & (q < LONG) & ((q < FULL) | (position[d] < 2))
-
-    def forwards(d, q):
-        return (position[d] == 0) | ((position[d] < HALF - 1) & (q < FULL))
-
-    def own_side(m, owner):
-        ref = wts.at[m, pl.ds(pl.multiple_of(owner * OLD, 16), OLD)]
-        return passing(ref, side_send, side_recv.at[m // 2], twin)
-
-    for copy in own:
-        copy.wait()
-
-    for d in range(2):
-        @pl.when(position[d] == 0)
-        def _():
-            @pl.loop(0, LONG)
-            def _(q):
-                cross(d, q).start()
-
-    def parcel(source, target, o, sender, receiver, device):
-        rows = pl.ds(pl.multiple_of(o * ROWS, ROWS), ROWS)
-        return pltpu.make_async_remote_copy(
-            src_ref=source.at[rows], dst_ref=target.at[rows], send_sem=sender, recv_sem=receiver.at[lax.div(o, BATCH)],
-            device_id=device, device_id_type=MESH,
-        )
-
-    def dispatch(o):
-        return parcel(send, recv, o, d_send, d_recv, peer(o, 1))
-
-    def give_back(o):
-        return parcel(outs, ret, o, r_send, r_recv, peer(o, -1))
-
-    def kept(source, target, receiver):
-        return pltpu.make_async_copy(source.at[0:ROWS], target.at[0:ROWS], receiver.at[0])
-
-    def landed(ref, receiver, i):
-        rows = batch_rows(i)
-        passing(ref.at[rows], d_send, receiver.at[i], twin).wait_recv()
-
-    def left(ref, sender):
-        passing(ref, sender, d_recv.at[0], twin).wait_send()
-
-    kept(send, recv, d_recv).start()
-
-    @pl.loop(1, BATCH)
-    def _(o):
-        dispatch(o).start()
-
-    for m in range(3):
-        own_side(m, low).start()
-
-    @pl.loop(1, EXPERTS // BATCH)
-    def _(i):
-        fill(i)
-
-    @pl.loop(0, FULL + SKEW * (HALF - 1))
+    @pl.loop(0, max(FULL + SKEW * (HALF - 1), LONG + SKEW))
     def _(j):
         for d in range(2):
             q = j - SKEW * position[d]
@@ -248,10 +253,14 @@
 
                 side(d, q, far).start()
 
-        @pl.when(j < (EXPERTS - BATCH) // 4)
+        @pl.when((j < PACE * (EXPERTS // BATCH - 1)) & (lax.rem(j, PACE) == 0))
         def _():
-            for o in range(4):
-                dispatch(BATCH + 4 * j + o).start()
+            i = lax.div(j, PACE) + 1
+            fill(i)
+
+            @pl.loop(0, BATCH)
+            def _(o):
+                dispatch(i * BATCH + o).start()
 
     def side_landed(i):
         rows = wts.at[0] if i == 0 else wts.at[0, 0 : UNITS // 2]
@@ -336,15 +345,15 @@
 
     left(send.at[0 : (EXPERTS - 1) * ROWS], d_send)
     left(wts.at[0:2, 0 : 3 * OLD], side_send)
-    for d in range(2):
-        @pl.when(position[d] == 0)
-        def _():
-            left(wts.at[0, 0 : LONG * PIECE], cross_send.at[d])
-            left(wts.at[0, 0 : LONG * PIECE], hop_send.at[d])
-
-        @pl.when((position[d] == 1) | (position[d] == 2))
-        def _():
-            left(wts.at[0, 0 : FULL * PIECE], hop_send.at[d])
+    @pl.when(position[0] == 0)
+    def _():
+        left(wts.at[0, 0 : LONG * PIECE], cross_send)
+        left(wts.at[0, 0 : LONG * PIECE], hop_send.at[0])
+
+    @pl.when(position[0] == 1)
+    def _():
+        left(wts.at[0, 0 : FULL * PIECE], hop_send.at[0])
+        left(wts.at[0, 0 : FULL * PIECE], hop_send.at[1])
 
     def sums(i, b):
         found = dot(lhs[b, :, batch_rows(i)], ret[batch_rows(i), b * Q : (b + 1) * Q])
@@ -415,7 +424,7 @@
             dma((EXPERTS // BATCH,)),
             dma,
             dma((EXPERTS // BATCH,)),
-            dma((2,)),
+            dma,
             dma((2,)),
             dma((2, LONG)),
             dma,

time: 93 us -> 93 us (level)
  no operation moved by 1% of the time
where the time goes in v5:
time: 93 us; the launch traced here: 91.2 us
  Pallas kernels  88.8 us (95%)
  local copies, waits for them, and re-layouts  1.81 us (2%)
    pallas_call x1, Pallas kernels, on_device(): pl.pallas_call(kernel, out_shape=(jax.ShapeDtypeStruct((TOK, D), BF16), j...  88.8 us

profile of v5, /device:TPU:1, one launch (start us, length us, event | category | flops | bytes accessed | tf_op | source)
XLA Modules:
  0.0 91.2 jit_solution(4279857724977709558)
XLA Ops:
  0.6 88.8 %moe.1 = (bf16[128,2048]{1,0:T(8,128)(2,1)S(1)}, bf16[3,96,2048]{2,1,0:T(8,128)(2,1)S(1)}) custom-call(bf16[128,2048]{1,0:T(8,128)(2,1)} %tokens.1, s32[8,128]{1,0:T(8,128)} %bitcast.4, f32[8,128]{1,0:T(8,128)} %bitcast.5, bf16[192,2048]{1,0:T(8,128)(2,1)} %gate.1, bf16[192,2048]{1,0:T(8,128)(2,1)} %up.1, bf16[192,2048]{1,0:T(8,128)(2,1)} %down.1, ...), custom_call_target="tpu_custom_call" | custom-call | tf_op jit(solution)/shard_map/moe/pallas_call | solution.py:397
  89.4 0.8 copy.11
  90.2 1.0 %copy.12 = bf16[3,96,2048]{2,1,0:T(8,128)(2,1)} copy(bf16[3,96,2048]{2,1,0:T(8,128)(2,1)S(1)} %get-tuple-element.5) | data formatting | bytes 2359296
